TPU v7x, 256 devices: a whole 4x4x8 slice. The times are simulated.
256 devices in a mesh: group: 16 (over y, x), ingroup: 16 (over z, core).
Axes of the slice: x: 4, y: 4, z: 8, core: 2. Of those that a mesh axis runs over, the one named last changes fastest.
Arguments:
- activations: bfloat16 [16384, 3584], P(('group', 'ingroup')), may hold values from -6 to 6
- gate_weights: bfloat16 [256, 1792, 1024], P(('group', 'ingroup')), may hold values from -0.09375 to 0.09375
- up_weights: bfloat16 [256, 1792, 1024], P(('group', 'ingroup')), may hold values from -0.09375 to 0.09375
- down_weights: bfloat16 [256, 1024, 1792], P(('group', 'ingroup')), may hold values from -0.375 to 0.375
- expert_ids: int32 [16384, 8], P(('group', 'ingroup')), may hold values from 0 to 127, as said below
- gate_scores: int32 [16384, 8], P(('group', 'ingroup')), may hold values from 1 to 15
- arrival_pos: int32 [16384], P(('group', 'ingroup')), may hold values from 0 to 63, as said below
Outputs:
- expert_mix: bfloat16 [16384, 3584], P(('group', 'ingroup'))
Inputs may be any that keep to these rules, and one draw needn't show every extreme that they name: `expert_ids`: each row names 8 different experts, two from each of 4 different groups. Among one device's 64 rows no expert is named more than 6 times and no group by more than 24 rows; on every device some expert is named exactly 6 times and some group by exactly 24 rows. `arrival_pos`: within each device's 64 rows the values are a permutation.
All inputs are finite; a program needn't handle non-finite values.
Results may differ from a plain program's by a relative error of at most 0.0077.
Values may be sent and summed in bfloat16 or wider, within the bound.
No kernel may reach another device: no remote copies, remote signals or barrier semaphores. Data moves between devices by JAX's collectives and lax.ppermute only.
A program may use at most 128 MiB of HBM per device.

v0:
```python
import jax
import jax.numpy as jnp
from jax import lax
from jax.sharding import PartitionSpec as P

TOPG = 4


def from_partner(shard, axis, apart):
    return lax.ppermute(shard, axis, [(i, i ^ 1 << apart) for i in range(lax.axis_size(axis))])


def group_layout(int_table, groups, members, expert_most):
    shaped = int_table.reshape(groups, members // 2, 1, expert_most)
    shaped = jnp.broadcast_to(shaped, (groups, members // 2, 2, expert_most))
    return shaped.reshape(groups, members, expert_most)


def per_device(
    activations, gate_weights, up_weights, down_weights, expert_ids, gate_scores, arrival_pos
):
    groups = lax.axis_size("group")
    members = lax.axis_size("ingroup")
    per_group = members // 2
    experts = groups * per_group
    tok_count = activations.shape[0]
    model_width = activations.shape[1]
    half_width = model_width // 2
    top_picks = expert_ids.shape[1]
    capacity = 2 * top_picks * tok_count
    group_most = min(tok_count, 3 * tok_count * TOPG // (2 * groups))
    expert_most = (2 * group_most + per_group - 1) // per_group
    expert_range = jnp.arange(experts, dtype=jnp.int32)
    pick_hits = (expert_ids[:, :, None] == expert_range[None, None, :]).astype(jnp.int32)
    hit_table = jnp.sum(pick_hits, axis=1)
    occurrence = jnp.cumsum(hit_table, axis=0) - hit_table
    position_range = jnp.arange(tok_count, dtype=jnp.int32)
    arrival_table = (arrival_pos[:, None] == position_range[None, :]).astype(jnp.int32)
    own_counts = jnp.dot(hit_table.T, arrival_table)
    shifts = jnp.arange(32, dtype=jnp.int32)
    flat_bits = own_counts.reshape(-1, 32)
    packed = jnp.sum(jnp.left_shift(flat_bits, shifts[None, :]), axis=1)[None, :]
    my_index = lax.axis_index(("group", "ingroup"))
    piece = lax.all_gather(packed, ("group", "ingroup"), axis=0, tiled=True)
    bit_table = jnp.bitwise_and(jnp.right_shift(piece[:, :, None], shifts[None, None, :]), 1)
    bit_table = bit_table.reshape(piece.shape[0], experts, tok_count)
    source_index = jnp.arange(piece.shape[0], dtype=jnp.int32)
    earlier_flag = (source_index < my_index).astype(jnp.int32)
    prior_part = jnp.sum(bit_table * earlier_flag[:, None, None], axis=0)
    total_part = jnp.sum(bit_table, axis=0)
    earlier = jnp.cumsum(total_part, axis=1) - total_part
    rank_table = earlier + prior_part
    rank_by_token = jnp.dot(arrival_table, rank_table.T)
    pick_rank = jnp.sum(pick_hits * rank_by_token[:, None, :], axis=2)
    pick_occurrence = jnp.sum(pick_hits * occurrence[:, None, :], axis=2)
    kept_mask = (pick_rank < capacity).astype(jnp.int32)
    kept_scores = gate_scores * kept_mask
    weight_sum = jnp.maximum(jnp.sum(kept_scores, axis=1), 1)
    routing = kept_scores.astype(jnp.float32) / weight_sum.astype(jnp.float32)[:, None]
    slot_range = jnp.arange(expert_most, dtype=jnp.int32)
    slot_match = hit_table[:, :, None] * (
        occurrence[:, :, None] == slot_range[None, None, :]
    ).astype(jnp.int32)
    slot_valid = jnp.sum(slot_match, axis=0)
    slot_token = jnp.sum(slot_match * position_range[:, None, None], axis=0)
    slot_rank = jnp.sum(slot_match * rank_by_token[:, :, None], axis=0)
    send_rank = jnp.where((slot_valid > 0) & (slot_rank < capacity), slot_rank, -1)
    half_index = jnp.arange(members, dtype=jnp.int32) % 2
    token_layout = jnp.transpose(group_layout(slot_token, groups, members, expert_most), (1, 0, 2))
    rank_layout = jnp.transpose(group_layout(send_rank, groups, members, expert_most), (1, 0, 2))
    feature_rows = activations.reshape(tok_count * 2, half_width)
    send_rows = jnp.take(feature_rows, token_layout * 2 + half_index[:, None, None], axis=0)
    got_rows, got_rank = (
        lax.all_to_all(
            lax.all_to_all(send_rows, "group", split_axis=1, concat_axis=1, tiled=True),
            "ingroup",
            split_axis=0,
            concat_axis=0,
            tiled=True,
        ),
        lax.all_to_all(
            lax.all_to_all(rank_layout, "group", split_axis=1, concat_axis=1, tiled=True),
            "ingroup",
            split_axis=0,
            concat_axis=0,
            tiled=True,
        ),
    )
    slot_total = members * groups * expert_most
    flat_rank = got_rank.reshape(slot_total)
    flat_rows = got_rows.reshape(slot_total, half_width)
    target = jnp.where(flat_rank >= 0, flat_rank, capacity)
    source_of = (
        jnp.zeros((capacity,), jnp.int32)
        .at[target]
        .set(jnp.arange(slot_total, dtype=jnp.int32), mode="drop")
    )
    filled = jnp.zeros((capacity,), jnp.bool_).at[target].set(True, mode="drop")
    expert_rows = jnp.where(
        filled[:, None], jnp.take(flat_rows, source_of, axis=0), jnp.zeros((), activations.dtype)
    )
    gate_part = jnp.dot(expert_rows, gate_weights[0], preferred_element_type=jnp.float32).astype(
        jnp.bfloat16
    )
    up_part = jnp.dot(expert_rows, up_weights[0], preferred_element_type=jnp.float32).astype(
        jnp.bfloat16
    )
    other_gate, other_up = from_partner((gate_part, up_part), "ingroup", 0)
    gate_sum = gate_part.astype(jnp.float32) + other_gate.astype(jnp.float32)
    up_sum = up_part.astype(jnp.float32) + other_up.astype(jnp.float32)
    hidden = (jax.nn.silu(gate_sum) * up_sum).astype(jnp.bfloat16)
    expert_out = jnp.dot(hidden, down_weights[0], preferred_element_type=jnp.float32).astype(
        jnp.bfloat16
    )
    back_rows = jnp.take(expert_out, jnp.clip(flat_rank, 0, capacity - 1), axis=0)
    back_rows = jnp.where((flat_rank >= 0)[:, None], back_rows, jnp.zeros((), jnp.bfloat16))
    back_rows = back_rows.reshape(members, groups, expert_most, half_width)
    pick_group = expert_ids // per_group
    returned = lax.all_to_all(
        lax.all_to_all(back_rows, "group", split_axis=1, concat_axis=1, tiled=True),
        "ingroup",
        split_axis=0,
        concat_axis=0,
        tiled=True,
    )
    pick_member = expert_ids % per_group * 2
    halves = jnp.arange(2, dtype=jnp.int32)
    flat_pick = (
        (pick_member[:, :, None] + halves[None, None, :]) * groups + pick_group[:, :, None]
    ) * expert_most + pick_occurrence[:, :, None]
    gathered = jnp.take(returned.reshape(slot_total, half_width), flat_pick, axis=0)
    terms = routing[:, :, None] * gathered.reshape(tok_count, top_picks, model_width).astype(
        jnp.float32
    )
    pick_range = jnp.arange(top_picks, dtype=jnp.int32)
    not_self = (pick_range[:, None] != pick_range[None, :]).astype(jnp.int32)
    same_other = (pick_group[:, :, None] == pick_group[:, None, :]).astype(jnp.int32) * not_self[
        None, :, :
    ]
    partner = jnp.sum(same_other * pick_range[None, None, :], axis=2)
    partner_terms = jnp.take_along_axis(terms, partner[:, :, None], axis=1)
    paired = terms + partner_terms
    rounded = lax.optimization_barrier(paired.astype(jnp.bfloat16)).astype(jnp.float32)
    combined = 0.5 * jnp.sum(rounded, axis=1)
    return combined.astype(jnp.bfloat16)


def solution(mesh):
    return jax.shard_map(
        per_device,
        mesh=mesh,
        in_specs=(
            P(("group", "ingroup"), None),
            P(("group", "ingroup"), None, None),
            P(("group", "ingroup"), None, None),
            P(("group", "ingroup"), None, None),
            P(("group", "ingroup"), None),
            P(("group", "ingroup"), None),
            P(("group", "ingroup")),
        ),
        out_specs=P(("group", "ingroup"), None),
        check_vma=False,
    )
```

profile of v0, /device:TPU:1, one launch (start us, length us, event | category | flops | bytes accessed | tf_op | source)
XLA Modules:
  0.0 716.8 jit_solution(8007721992500397717)
XLA Ops:
  0.0 0.8 copy.125
  0.8 0.1 convert_reduce_fusion.1
  1.0 0.9 fusion.22
  2.0 0.1 shift-left_reduce_fusion
  2.1 67.0 %all-gather.1 = s32[256,1,256]{2,1,0:T(1,128)S(1)} all-gather(s32[1,1,256]{2,1,0:T(1,128)S(1)} %bitcast.53), channel_id=2, replica_groups=mesh['group'=16,'ingroup'=16] {'group','ingroup'}, dimensions={0}, use_global_device_ids=true | all-gather | bytes 263168 | tf_op jit(solution)/shard_map/all_gather | solution.py:44
  69.2 1.7 fusion
  71.2 0.1 reduce_window_sum.23
  71.7 0.9 fusion.19
  72.9 0.7 copy.142
  73.7 4.2 all-to-all-start
  78.3 0.2 copy.149
  78.4 0.1 reshape.254
  78.6 0.2 reshape.248
  78.8 6.7 gather_fusion
  85.5 9.6 %reshape.253 = bf16[16,16,6,1792]{3,2,1,0:T(8,128)(2,1)} reshape(bf16[1536,1792]{1,0:T(8,128)(2,1)} %gather_fusion) | data formatting | bytes 11010048 | tf_op jit(solution)/shard_map/jit(_take)/gather | solution.py:72
  95.1 0.2 copy.148
  95.3 4.0 broadcast_select_fusion
  99.3 5.5 copy.150
  104.8 6.7 all-to-all-start.2
  111.5 0.7 copy.143
  112.2 80.3 %all-to-all-done.2 = bf16[16,16,6,1792]{3,0,2,1:T(8,128)(2,1)} async-done(((bf16[16,16,6,1792]{3,0,2,1:T(8,128)(2,1)}), bf16[16,16,6,1792]{3,0,2,1:T(8,128)(2,1)}, u32[]{:S(2)}, u32[]{:S(2)}) %all-to-all-start.2) | async-done | bytes 5505056 | tf_op jit(solution)/shard_map/all_to_all | solution.py:75
  192.5 6.3 all-to-all-start.1
  198.8 7.9 %copy.151 = bf16[16,16,6,1792]{3,1,2,0:T(8,128)(2,1)} copy(bf16[16,16,6,1792]{3,0,2,1:T(8,128)(2,1)} %all-to-all-done.2) | data formatting | bytes 11010048 | tf_op jit(solution)/shard_map/all_to_all | solution.py:75
  206.7 7.2 %all-to-all-start.3 = ((bf16[16,16,6,1792]{3,1,2,0:T(8,128)(2,1)}), bf16[16,16,6,1792]{3,1,2,0:T(8,128)(2,1)}, u32[]{:S(2)}, u32[]{:S(2)}) async-start(bf16[16,16,6,1792]{3,1,2,0:T(8,128)(2,1)} %copy.151), calls=%async_computation.3 | async-start | bytes 11010048 | tf_op jit(solution)/shard_map/all_to_all | solution.py:74
  213.9 0.2 copy.146
  214.1 0.1 reshape.247
  214.3 6.2 scatter_custom_fusion.1
  220.5 11.6 %scatter_custom_fusion = pred[1024]{0:T(1024)(128)(4,1)S(1)} fusion(s32[1536]{0:T(1024)S(1)} %get-tuple-element.13, pred[1536]{0:T(1024)(128)(4,1)S(1)} %broadcast.331, pred[]{:T(512)} %constant.148.clone.1), kind=kCustom, calls=%fused_computation.100 | custom fusion | bytes 1025 | tf_op jit(solution)/shard_map/scatter | solution.py:98
  232.2 103.5 %all-to-all-done.3 = bf16[16,16,6,1792]{3,1,2,0:T(8,128)(2,1)} async-done(((bf16[16,16,6,1792]{3,1,2,0:T(8,128)(2,1)}), bf16[16,16,6,1792]{3,1,2,0:T(8,128)(2,1)}, u32[]{:S(2)}, u32[]{:S(2)}) %all-to-all-start.3) | async-done | bytes 5505056 | tf_op jit(solution)/shard_map/all_to_all | solution.py:74
  335.7 7.7 %copy.152 = bf16[16,16,6,1792]{3,2,1,0:T(8,128)(2,1)} copy(bf16[16,16,6,1792]{3,1,2,0:T(8,128)(2,1)} %all-to-all-done.3) | data formatting | bytes 11010048 | tf_op jit(solution)/shard_map/all_to_all | solution.py:74
  343.3 9.7 %reshape.249 = bf16[1536,1792]{1,0:T(8,128)(2,1)} reshape(bf16[16,16,6,1792]{3,2,1,0:T(8,128)(2,1)} %copy.152) | data formatting | bytes 11010048 | tf_op jit(solution)/shard_map/reshape | solution.py:91
  353.0 11.2 %gather_fusion.1 = bf16[1024,1792]{1,0:T(8,128)(2,1)} fusion(bf16[1536,1792]{1,0:T(8,128)(2,1)} %reshape.249, s32[1024]{0:T(1024)S(1)} %fusion.37), kind=kCustom, calls=%fused_computation.1 | custom fusion | bytes 7344128 | tf_op jit(solution)/shard_map/jit(_take)/gather | solution.py:100
  364.2 7.3 %fusion.10 = bf16[1024,1024]{1,0:T(8,128)(2,1)S(1)} fusion(bf16[1,1792,1024]{2,1,0:T(8,128)(2,1)} %param.8, bf16[1024,1792]{1,0:T(8,128)(2,1)} %gather_fusion.1, pred[1024]{0:T(1024)(128)(4,1)S(1)} %compare_and_fusion.3, pred[1024]{0:T(1024)(128)(4,1)S(1)} %scatter_custom_fusion), kind=kOutput, calls=%fused_computation.28 | convolution fusion | flops 3762814976 | bytes 9439232 | tf_op jit(solution)/shard_map/dot_general | solution.py:102
  371.5 1.0 collective-permute-start
  372.5 5.6 fusion.13
  378.1 0.2 collective-permute-start.1
  378.3 0.2 copy.144
  378.5 0.2 copy.145
  378.7 4.0 collective-permute-done.1
  382.7 10.9 %convolution_convert_fusion = bf16[1024,1792]{1,0:T(8,128)(2,1)} fusion(bf16[1,1024,1792]{2,1,0:T(8,128)(2,1)} %param.10, bf16[1024,1024]{1,0:T(8,128)(2,1)} %collective-permute-done.1, bf16[1024,1024]{1,0:T(8,128)(2,1)} %fusion.13, bf16[1024,1024]{1,0:T(8,128)(2,1)} %collective-permute-done, bf16[1024,1024]{1,0:T(8,128)(2,1)S(1)} %fusion.10), kind=kOutput, calls=%fused_computation.18 | convolution fusion | flops 3772514304 | bytes 15728640 | tf_op jit(solution)/shard_map/dot_general | solution.py:112
  393.6 13.9 %gather_fusion.2 = bf16[1536,1792]{1,0:T(8,128)(2,1)} fusion(bf16[1024,1792]{1,0:T(8,128)(2,1)} %convolution_convert_fusion, s32[2048]{0:T(1024)S(1)} %pad_clamp_fusion), kind=kCustom, calls=%fused_computation.2 | custom fusion | bytes 11016192 | tf_op jit(solution)/shard_map/jit(_take)/gather | solution.py:115
  407.5 9.6 %gather.25 = bf16[16,16,6,1792]{3,2,1,0:T(8,128)(2,1)} reshape(bf16[1536,1792]{1,0:T(8,128)(2,1)} %gather_fusion.2) | data formatting | bytes 11010048 | tf_op jit(solution)/shard_map/jit(_take)/gather | solution.py:115
  417.1 4.4 select_select_fusion
  421.5 3.0 copy.153
  424.5 69.9 %all_to_all.30 = bf16[16,16,6,1792]{3,0,2,1:T(8,128)(2,1)S(1)} all-to-all(bf16[16,16,6,1792]{3,0,2,1:T(8,128)(2,1)S(1)} %copy.153), channel_id=1, replica_groups=mesh['group'=16,'ingroup'=16] {'group'}, dimensions={1} | all-to-all | bytes 11010048 | tf_op jit(solution)/shard_map/all_to_all | solution.py:120
  494.4 5.4 copy.154
  499.8 6.2 all-to-all-start.5
  506.0 2.3 select_reduce_fusion.2
  508.6 0.3 compare_select_fusion
  508.9 0.2 reshape.278
  509.0 0.2 copy.140
  509.8 0.1 copy.160
  510.2 117.6 %all-to-all-done.5 = bf16[16,16,6,1792]{3,1,2,0:T(8,128)(2,1)} async-done(((bf16[16,16,6,1792]{3,1,2,0:T(8,128)(2,1)}), bf16[16,16,6,1792]{3,1,2,0:T(8,128)(2,1)}, u32[]{:S(2)}, u32[]{:S(2)}) %all-to-all-start.5) | async-done | bytes 5505056 | tf_op jit(solution)/shard_map/all_to_all | solution.py:119
  627.7 7.7 %copy.155 = bf16[16,16,6,1792]{3,2,1,0:T(8,128)(2,1)} copy(bf16[16,16,6,1792]{3,1,2,0:T(8,128)(2,1)} %all-to-all-done.5) | data formatting | bytes 11010048 | tf_op jit(solution)/shard_map/all_to_all | solution.py:119
  635.4 9.7 %reshape.250 = bf16[1536,1792]{1,0:T(8,128)(2,1)} reshape(bf16[16,16,6,1792]{3,2,1,0:T(8,128)(2,1)} %copy.155) | data formatting | bytes 11010048 | tf_op jit(solution)/shard_map/reshape | solution.py:131
  645.1 11.2 %gather_fusion.3 = bf16[1024,1792]{1,0:T(8,128)(2,1)} fusion(bf16[1536,1792]{1,0:T(8,128)(2,1)} %reshape.250, s32[1024]{0:T(1024)S(1)} %broadcast_clamp_fusion), kind=kCustom, calls=%fused_computation.3 | custom fusion | bytes 7344128 | tf_op jit(solution)/shard_map/jit(_take)/gather | solution.py:131
  656.3 8.6 %reshape.277 = bf16[64,8,2,1792]{3,2,1,0:T(2,128)(2,1)} reshape(bf16[1024,1792]{1,0:T(8,128)(2,1)} %gather_fusion.3) | data formatting | bytes 7340032 | tf_op jit(solution)/shard_map/jit(_take)/gather | solution.py:131
  664.9 8.5 %fusion.3 = f32[64,8,2,1792]{3,2,1,0:T(2,128)} fusion(bf16[64,8,2,1792]{3,2,1,0:T(2,128)(2,1)} %reshape.277, pred[64,8,2]{2,1,0:T(8,128)(4,1)S(1)} %copy.140), kind=kLoop, calls=%fused_computation.19 | loop fusion | flops 3670016 | bytes 11011072 | tf_op jit(solution)/shard_map/convert_element_type | solution.py:132
  673.4 10.0 %reshape.251 = f32[64,8,3584]{2,1,0:T(8,128)} reshape(f32[64,8,2,1792]{3,2,1,0:T(2,128)} %fusion.3) | data formatting | bytes 14680064 | tf_op jit(solution)/shard_map/convert_element_type | solution.py:132
  683.4 6.9 broadcast_multiply_fusion
  690.3 16.6 %gather_fusion.4 = f32[512,3584]{1,0:T(8,128)} fusion(f32[64,8,3584]{2,1,0:T(8,128)} %broadcast_multiply_fusion, s32[512]{0:T(512)S(1)} %reshape.284), kind=kCustom, calls=%fused_computation.4 | custom fusion | bytes 14684160 | tf_op jit(solution)/shard_map/jit(take_along_axis)/gather | solution.py:141
  706.9 6.2 fusion.2
  713.1 2.4 convert_reduce_fusion
  715.5 0.8 multiply_convert_fusion.2
  (63 shorter events, 2.6 us)
Async XLA Ops:
  0.0 78.6 %copy-start.1 = (bf16[64,3584]{1,0:T(8,128)(2,1)S(1)}, bf16[64,3584]{1,0:T(8,128)(2,1)}, u32[]{:S(2)}) copy-start(bf16[64,3584]{1,0:T(8,128)(2,1)} %param.7) | copy-start | bytes 1376260
  73.7 31.1 %all-to-all-start = ((s32[16,16,6]{0,2,1:T(8,128)}), s32[16,16,6]{0,2,1:T(8,128)S(1)}, u32[]{:S(2)}, u32[]{:S(2)}) async-start(s32[16,16,6]{0,2,1:T(8,128)} %copy.142), calls=%async_computation | async-start | bytes 131072 | tf_op jit(solution)/shard_map/all_to_all | solution.py:82
  104.8 87.7 %all-to-all-start.2 = ((bf16[16,16,6,1792]{3,0,2,1:T(8,128)(2,1)}), bf16[16,16,6,1792]{3,0,2,1:T(8,128)(2,1)}, u32[]{:S(2)}, u32[]{:S(2)}) async-start(bf16[16,16,6,1792]{3,0,2,1:T(8,128)(2,1)} %copy.150), calls=%async_computation.2 | async-start | bytes 11010048 | tf_op jit(solution)/shard_map/all_to_all | solution.py:75
  192.5 14.2 %all-to-all-start.1 = ((s32[16,16,6]{1,2,0:T(8,128)}), s32[16,16,6]{1,2,0:T(8,128)S(1)}, u32[]{:S(2)}, u32[]{:S(2)}) async-start(s32[16,16,6]{1,2,0:T(8,128)} %copy.143), calls=%async_computation.1 | async-start | bytes 131072 | tf_op jit(solution)/shard_map/all_to_all | solution.py:81
  206.7 129.0 %all-to-all-start.3 = ((bf16[16,16,6,1792]{3,1,2,0:T(8,128)(2,1)}), bf16[16,16,6,1792]{3,1,2,0:T(8,128)(2,1)}, u32[]{:S(2)}, u32[]{:S(2)}) async-start(bf16[16,16,6,1792]{3,1,2,0:T(8,128)(2,1)} %copy.151), calls=%async_computation.3 | async-start | bytes 11010048 | tf_op jit(solution)/shard_map/all_to_all | solution.py:74
  364.2 8.3 %copy-start = (bf16[1024,1792]{1,0:T(8,128)(2,1)S(1)}, bf16[1024,1792]{1,0:T(8,128)(2,1)}, u32[]{:S(2)}) copy-start(bf16[1024,1792]{1,0:T(8,128)(2,1)} %gather_fusion.1) | copy-start | bytes 11010052
  364.2 8.3 %copy-start.3 = (bf16[1,1792,1024]{2,1,0:T(8,128)(2,1)S(1)}, bf16[1,1792,1024]{2,1,0:T(8,128)(2,1)}, u32[]{:S(2)}) copy-start(bf16[1,1792,1024]{2,1,0:T(8,128)(2,1)} %param.9) | copy-start | bytes 11010052
  371.5 7.2 %collective-permute-start = (bf16[1024,1024]{1,0:T(8,128)(2,1)S(1)}, bf16[1024,1024]{1,0:T(8,128)(2,1)}, u32[]{:S(2)}, u32[]{:S(2)}) collective-permute-start(bf16[1024,1024]{1,0:T(8,128)(2,1)S(1)} %fusion.10), channel_id=1, source_target_pairs={{0,1},{1,0},{2,3},{3,2},{4,5},{5,4},{6,7},{7,6},{8,9},{9,8},{10,11... | collective-permute-start | bytes 6291464 | tf_op jit(solution)/shard_map/ppermute | solution.py:10
  378.1 4.7 collective-permute-start.1
  499.8 9.5 %copy-start.2 = (s32[64,8]{0,1:T(8,128)S(1)}, s32[64,8]{0,1:T(8,128)}, u32[]{:S(2)}) copy-start(s32[64,8]{0,1:T(8,128)} %param.12) | copy-start | bytes 6148
  499.8 128.0 %all-to-all-start.5 = ((bf16[16,16,6,1792]{3,1,2,0:T(8,128)(2,1)}), bf16[16,16,6,1792]{3,1,2,0:T(8,128)(2,1)}, u32[]{:S(2)}, u32[]{:S(2)}) async-start(bf16[16,16,6,1792]{3,1,2,0:T(8,128)(2,1)} %copy.154), calls=%async_computation.5 | async-start | bytes 11010048 | tf_op jit(solution)/shard_map/all_to_all | solution.py:119
where the time goes:
time: 726 us; the launch traced here: 717 us
  waiting for transfers between devices  305 us (42%)
  local copies, waits for them, and re-layouts  177 us (24%)
  blocking collectives  137 us (19%)
  other arithmetic  38.8 us (5%)
  starting transfers between devices  31.8 us (4%)
  matrix products  25.6 us (4%)
    all_to_all x1, waiting for transfers between devices, per_device(): lax.all_to_all(lax.all_to_all(back_rows, 'group', split_axis=1, concat_ax...  118 us
    all_to_all x1, waiting for transfers between devices, per_device(): lax.all_to_all(lax.all_to_all(send_rows, 'group', split_axis=1, concat_ax...  104 us
    all_to_all x1, waiting for transfers between devices, per_device(): lax.all_to_all(send_rows, 'group', split_axis=1, concat_axis=1, tiled=True)  80.3 us
    all_to_all x1, blocking collectives, per_device(): lax.all_to_all(back_rows, 'group', split_axis=1, concat_axis=1, tiled=True)  69.9 us
    all_gather x1, blocking collectives, per_device(): piece = lax.all_gather(packed, ('group', 'ingroup'), axis=0, tiled=True)  67 us
    gather x2, local copies, waits for them, and re-layouts, per_device(): jnp.take(expert_out, jnp.clip(flat_rank, 0, capacity - 1), axis=0)  23.4 us
    gather x2, local copies, waits for them, and re-layouts, per_device(): jnp.take(returned.reshape(slot_total, half_width), flat_pick, axis=0)  19.8 us
    gather x3, local copies, waits for them, and re-layouts, per_device(): partner_terms = jnp.take_along_axis(terms, partner[:, :, None], axis=1)  16.8 us
  transfers between devices with their start and end apart: 7, of which 4 were waited for; matrix products, arithmetic and copies ran while one was open for 9% of the time, Pallas kernels for 0%

commit v1 on v0

--- a/solution.py
+++ b/solution.py
@@ -4,6 +4,11 @@
 from jax.sharding import PartitionSpec as P
 
 TOPG = 4
+
+
+def exchange_gather(x, axis, along):
+    sent = jnp.stack([x] * lax.axis_size(axis))
+    return jnp.concatenate(lax.all_to_all(sent, axis, 0, 0), axis=along)
 
 
 def from_partner(shard, axis, apart):
@@ -41,7 +46,7 @@
     flat_bits = own_counts.reshape(-1, 32)
     packed = jnp.sum(jnp.left_shift(flat_bits, shifts[None, :]), axis=1)[None, :]
     my_index = lax.axis_index(("group", "ingroup"))
-    piece = lax.all_gather(packed, ("group", "ingroup"), axis=0, tiled=True)
+    piece = exchange_gather(packed, ("group", "ingroup"), 0)
     bit_table = jnp.bitwise_and(jnp.right_shift(piece[:, :, None], shifts[None, None, :]), 1)
     bit_table = bit_table.reshape(piece.shape[0], experts, tok_count)
     source_index = jnp.arange(piece.shape[0], dtype=jnp.int32)

time: 726 us -> 689 us (0.949)
  blocking collectives: 137 us -> 69.8 us
  waiting for transfers between devices: 305 us -> 320 us
  starting transfers between devices: 31.8 us -> 46 us
    all_gather x1 -> x0, blocking collectives: 67 us -> none  [per_device(): piece = lax.all_gather(packed, ('group', 'ingroup'), axis=0, tiled=True)]
    all_to_all x0 -> x1, starting transfers between devices: none -> 15.7 us  [exchange_gather(): return jnp.concatenate(lax.all_to_all(sent, axis, 0, 0), axis=along)]
    all_to_all x0 -> x1, waiting for transfers between devices: none -> 14.6 us  [exchange_gather(): return jnp.concatenate(lax.all_to_all(sent, axis, 0, 0), axis=along)]
  transfers between devices with their start and end apart: 7 -> 8, of which waited for: 4 -> 5; matrix products, arithmetic and copies ran while one was open for 9% -> 7% of each run, Pallas kernels for 0% -> 0%
where the time goes in v1:
time: 689 us; the launch traced here: 679 us
  waiting for transfers between devices  320 us (46%)
  local copies, waits for them, and re-layouts  179 us (26%)
  blocking collectives  69.8 us (10%)
  starting transfers between devices  46 us (7%)
  other arithmetic  38.8 us (6%)
  matrix products  24.9 us (4%)
    all_to_all x1, waiting for transfers between devices, per_device(): lax.all_to_all(lax.all_to_all(back_rows, 'group', split_axis=1, concat_ax...  118 us
    all_to_all x1, waiting for transfers between devices, per_device(): lax.all_to_all(lax.all_to_all(send_rows, 'group', split_axis=1, concat_ax...  104 us
    all_to_all x1, waiting for transfers between devices, per_device(): lax.all_to_all(send_rows, 'group', split_axis=1, concat_axis=1, tiled=True)  80.2 us
    all_to_all x1, blocking collectives, per_device(): lax.all_to_all(back_rows, 'group', split_axis=1, concat_axis=1, tiled=True)  69.8 us
    gather x2, local copies, waits for them, and re-layouts, per_device(): jnp.take(expert_out, jnp.clip(flat_rank, 0, capacity - 1), axis=0)  23.4 us
    gather x2, local copies, waits for them, and re-layouts, per_device(): jnp.take(returned.reshape(slot_total, half_width), flat_pick, axis=0)  19.8 us
    gather x3, local copies, waits for them, and re-layouts, per_device(): partner_terms = jnp.take_along_axis(terms, partner[:, :, None], axis=1)  16.8 us
    gather x2, local copies, waits for them, and re-layouts, per_device(): jnp.take(feature_rows, token_layout * 2 + half_index[:, None, None], axis=0)  16.3 us
  transfers between devices with their start and end apart: 8, of which 5 were waited for; matrix products, arithmetic and copies ran while one was open for 7% of the time, Pallas kernels for 0%

profile of v1, /device:TPU:1, one launch (start us, length us, event | category | flops | bytes accessed | tf_op | source)
XLA Modules:
  0.0 679.5 jit_solution(15337387334209456265)
XLA Ops:
  0.0 0.8 copy.160
  0.8 0.1 convert_reduce_fusion.1
  0.9 0.9 fusion.22
  2.1 0.9 stack.3
  2.9 15.7 %all-to-all-start = ((s32[256,1,256]{2,1,0:T(1,128)}), s32[256,1,256]{2,1,0:T(1,128)S(1)}, u32[]{:S(2)}, u32[]{:S(2)}) async-start(s32[256,1,256]{2,1,0:T(1,128)} %stack.3), calls=%async_computation | async-start | bytes 524288 | tf_op jit(solution)/shard_map/all_to_all | solution.py:11
  18.7 1.2 reshape.250
  19.9 14.6 %all-to-all-done = s32[256,1,256]{2,1,0:T(1,128)S(1)} async-done(((s32[256,1,256]{2,1,0:T(1,128)}), s32[256,1,256]{2,1,0:T(1,128)S(1)}, u32[]{:S(2)}, u32[]{:S(2)}) %all-to-all-start) | async-done | bytes 262176 | tf_op jit(solution)/shard_map/all_to_all | solution.py:11
  34.5 1.7 fusion
  36.5 0.1 reduce_window_sum.22
  36.9 0.2 fusion.19
  37.6 0.2 copy.184
  37.7 0.1 reshape.256
  37.9 6.7 gather_fusion
  44.6 9.6 %reshape.255 = bf16[16,16,6,1792]{3,2,1,0:T(8,128)(2,1)} reshape(bf16[1536,1792]{1,0:T(8,128)(2,1)} %gather_fusion) | data formatting | bytes 11010048 | tf_op jit(solution)/shard_map/jit(_take)/gather | solution.py:77
  54.2 0.2 copy.183
  54.7 0.7 copy.177
  55.5 3.5 all-to-all-start.1
  59.0 4.0 broadcast_select_fusion
  63.0 5.5 copy.185
  68.5 6.6 all-to-all-start.3
  75.1 0.7 copy.178
  75.8 80.2 %all-to-all-done.3 = bf16[16,16,6,1792]{3,0,2,1:T(8,128)(2,1)} async-done(((bf16[16,16,6,1792]{3,0,2,1:T(8,128)(2,1)}), bf16[16,16,6,1792]{3,0,2,1:T(8,128)(2,1)}, u32[]{:S(2)}, u32[]{:S(2)}) %all-to-all-start.3) | async-done | bytes 5505056 | tf_op jit(solution)/shard_map/all_to_all | solution.py:80
  156.0 5.5 all-to-all-start.2
  161.6 7.9 %copy.186 = bf16[16,16,6,1792]{3,1,2,0:T(8,128)(2,1)} copy(bf16[16,16,6,1792]{3,0,2,1:T(8,128)(2,1)} %all-to-all-done.3) | data formatting | bytes 11010048 | tf_op jit(solution)/shard_map/all_to_all | solution.py:80
  169.5 7.3 %all-to-all-start.4 = ((bf16[16,16,6,1792]{3,1,2,0:T(8,128)(2,1)}), bf16[16,16,6,1792]{3,1,2,0:T(8,128)(2,1)}, u32[]{:S(2)}, u32[]{:S(2)}) async-start(bf16[16,16,6,1792]{3,1,2,0:T(8,128)(2,1)} %copy.186), calls=%async_computation.4 | async-start | bytes 11010048 | tf_op jit(solution)/shard_map/all_to_all | solution.py:79
  176.8 0.2 copy.181
  176.9 0.1 reshape.249
  177.1 6.2 scatter_custom_fusion.1
  183.3 11.6 %scatter_custom_fusion = pred[1024]{0:T(1024)(128)(4,1)S(1)} fusion(s32[1536]{0:T(1024)S(1)} %get-tuple-element.13, pred[1536]{0:T(1024)(128)(4,1)S(1)} %broadcast.332, pred[]{:T(512)} %constant.148.clone.1), kind=kCustom, calls=%fused_computation.100 | custom fusion | bytes 1025 | tf_op jit(solution)/shard_map/scatter | solution.py:103
  195.0 103.5 %all-to-all-done.4 = bf16[16,16,6,1792]{3,1,2,0:T(8,128)(2,1)} async-done(((bf16[16,16,6,1792]{3,1,2,0:T(8,128)(2,1)}), bf16[16,16,6,1792]{3,1,2,0:T(8,128)(2,1)}, u32[]{:S(2)}, u32[]{:S(2)}) %all-to-all-start.4) | async-done | bytes 5505056 | tf_op jit(solution)/shard_map/all_to_all | solution.py:79
  298.5 7.7 %copy.187 = bf16[16,16,6,1792]{3,2,1,0:T(8,128)(2,1)} copy(bf16[16,16,6,1792]{3,1,2,0:T(8,128)(2,1)} %all-to-all-done.4) | data formatting | bytes 11010048 | tf_op jit(solution)/shard_map/all_to_all | solution.py:79
  306.2 9.7 %reshape.251 = bf16[1536,1792]{1,0:T(8,128)(2,1)} reshape(bf16[16,16,6,1792]{3,2,1,0:T(8,128)(2,1)} %copy.187) | data formatting | bytes 11010048 | tf_op jit(solution)/shard_map/reshape | solution.py:96
  315.8 11.2 %gather_fusion.1 = bf16[1024,1792]{1,0:T(8,128)(2,1)} fusion(bf16[1536,1792]{1,0:T(8,128)(2,1)} %reshape.251, s32[1024]{0:T(1024)S(1)} %fusion.37), kind=kCustom, calls=%fused_computation.1 | custom fusion | bytes 7344128 | tf_op jit(solution)/shard_map/jit(_take)/gather | solution.py:105
  327.0 7.3 %fusion.10 = bf16[1024,1024]{1,0:T(8,128)(2,1)S(1)} fusion(bf16[1,1792,1024]{2,1,0:T(8,128)(2,1)} %param.8, bf16[1024,1792]{1,0:T(8,128)(2,1)} %gather_fusion.1, pred[1024]{0:T(1024)(128)(4,1)S(1)} %compare_and_fusion.3, pred[1024]{0:T(1024)(128)(4,1)S(1)} %scatter_custom_fusion), kind=kOutput, calls=%fused_computation.28 | convolution fusion | flops 3762814976 | bytes 9439232 | tf_op jit(solution)/shard_map/dot_general | solution.py:107
  334.3 1.0 collective-permute-start
  335.3 5.6 fusion.13
  340.9 0.2 collective-permute-start.1
  341.1 0.2 copy.179
  341.3 0.2 copy.180
  341.6 4.0 collective-permute-done.1
  345.5 10.8 %convolution_convert_fusion = bf16[1024,1792]{1,0:T(8,128)(2,1)} fusion(bf16[1,1024,1792]{2,1,0:T(8,128)(2,1)} %param.10, bf16[1024,1024]{1,0:T(8,128)(2,1)} %collective-permute-done.1, bf16[1024,1024]{1,0:T(8,128)(2,1)} %fusion.13, bf16[1024,1024]{1,0:T(8,128)(2,1)} %collective-permute-done, bf16[1024,1024]{1,0:T(8,128)(2,1)S(1)} %fusion.10), kind=kOutput, calls=%fused_computation.18 | convolution fusion | flops 3772514304 | bytes 15728640 | tf_op jit(solution)/shard_map/dot_general | solution.py:117
  356.4 13.9 %gather_fusion.2 = bf16[1536,1792]{1,0:T(8,128)(2,1)} fusion(bf16[1024,1792]{1,0:T(8,128)(2,1)} %convolution_convert_fusion, s32[2048]{0:T(1024)S(1)} %pad_clamp_fusion), kind=kCustom, calls=%fused_computation.2 | custom fusion | bytes 11016192 | tf_op jit(solution)/shard_map/jit(_take)/gather | solution.py:120
  370.2 9.6 %gather.25 = bf16[16,16,6,1792]{3,2,1,0:T(8,128)(2,1)} reshape(bf16[1536,1792]{1,0:T(8,128)(2,1)} %gather_fusion.2) | data formatting | bytes 11010048 | tf_op jit(solution)/shard_map/jit(_take)/gather | solution.py:120
  379.8 4.4 select_select_fusion
  384.2 3.0 copy.188
  387.2 69.8 %all_to_all.35 = bf16[16,16,6,1792]{3,0,2,1:T(8,128)(2,1)S(1)} all-to-all(bf16[16,16,6,1792]{3,0,2,1:T(8,128)(2,1)S(1)} %copy.188), channel_id=1, replica_groups=mesh['group'=16,'ingroup'=16] {'group'}, dimensions={1} | all-to-all | bytes 11010048 | tf_op jit(solution)/shard_map/all_to_all | solution.py:125
  457.0 5.4 copy.189
  462.5 6.3 all-to-all-start.6
  469.6 2.3 select_reduce_fusion.2
  472.0 0.3 compare_select_fusion
  472.2 0.2 reshape.280
  472.4 0.2 copy.175
  472.9 117.6 %all-to-all-done.6 = bf16[16,16,6,1792]{3,1,2,0:T(8,128)(2,1)} async-done(((bf16[16,16,6,1792]{3,1,2,0:T(8,128)(2,1)}), bf16[16,16,6,1792]{3,1,2,0:T(8,128)(2,1)}, u32[]{:S(2)}, u32[]{:S(2)}) %all-to-all-start.6) | async-done | bytes 5505056 | tf_op jit(solution)/shard_map/all_to_all | solution.py:124
  590.4 7.7 %copy.190 = bf16[16,16,6,1792]{3,2,1,0:T(8,128)(2,1)} copy(bf16[16,16,6,1792]{3,1,2,0:T(8,128)(2,1)} %all-to-all-done.6) | data formatting | bytes 11010048 | tf_op jit(solution)/shard_map/all_to_all | solution.py:124
  598.1 9.7 %reshape.252 = bf16[1536,1792]{1,0:T(8,128)(2,1)} reshape(bf16[16,16,6,1792]{3,2,1,0:T(8,128)(2,1)} %copy.190) | data formatting | bytes 11010048 | tf_op jit(solution)/shard_map/reshape | solution.py:136
  607.8 11.2 %gather_fusion.3 = bf16[1024,1792]{1,0:T(8,128)(2,1)} fusion(bf16[1536,1792]{1,0:T(8,128)(2,1)} %reshape.252, s32[1024]{0:T(1024)S(1)} %broadcast_clamp_fusion), kind=kCustom, calls=%fused_computation.3 | custom fusion | bytes 7344128 | tf_op jit(solution)/shard_map/jit(_take)/gather | solution.py:136
  619.0 8.6 %reshape.279 = bf16[64,8,2,1792]{3,2,1,0:T(2,128)(2,1)} reshape(bf16[1024,1792]{1,0:T(8,128)(2,1)} %gather_fusion.3) | data formatting | bytes 7340032 | tf_op jit(solution)/shard_map/jit(_take)/gather | solution.py:136
  627.6 8.5 %fusion.3 = f32[64,8,2,1792]{3,2,1,0:T(2,128)} fusion(bf16[64,8,2,1792]{3,2,1,0:T(2,128)(2,1)} %reshape.279, pred[64,8,2]{2,1,0:T(8,128)(4,1)S(1)} %copy.175), kind=kLoop, calls=%fused_computation.19 | loop fusion | flops 3670016 | bytes 11011072 | tf_op jit(solution)/shard_map/convert_element_type | solution.py:137
  636.1 10.0 %reshape.253 = f32[64,8,3584]{2,1,0:T(8,128)} reshape(f32[64,8,2,1792]{3,2,1,0:T(2,128)} %fusion.3) | data formatting | bytes 14680064 | tf_op jit(solution)/shard_map/convert_element_type | solution.py:137
  646.1 6.9 %broadcast_multiply_fusion = f32[64,8,3584]{2,1,0:T(8,128)} fusion(f32[64,8,3584]{2,1,0:T(8,128)} %reshape.253, f32[64,8]{1,0:T(8,128)S(1)} %convert_divide_fusion), kind=kLoop, calls=%fused_computation.26 | loop fusion | flops 1835008 | bytes 14682112 | tf_op jit(solution)/shard_map/mul | solution.py:137
  653.0 16.6 %gather_fusion.4 = f32[512,3584]{1,0:T(8,128)} fusion(f32[64,8,3584]{2,1,0:T(8,128)} %broadcast_multiply_fusion, s32[512]{0:T(512)S(1)} %reshape.286), kind=kCustom, calls=%fused_computation.4 | custom fusion | bytes 14684160 | tf_op jit(solution)/shard_map/jit(take_along_axis)/gather | solution.py:146
  669.6 6.2 fusion.2
  675.8 2.4 convert_reduce_fusion
  678.2 0.8 multiply_convert_fusion.2
  (65 shorter events, 2.8 us)
Async XLA Ops:
  0.0 36.9 %copy-start.2 = (s32[64]{0:T(128)S(1)}, s32[64]{0:T(128)}, u32[]{:S(2)}) copy-start(s32[64]{0:T(128)} %param.13) | copy-start | bytes 772
  2.9 31.6 %all-to-all-start = ((s32[256,1,256]{2,1,0:T(1,128)}), s32[256,1,256]{2,1,0:T(1,128)S(1)}, u32[]{:S(2)}, u32[]{:S(2)}) async-start(s32[256,1,256]{2,1,0:T(1,128)} %stack.3), calls=%async_computation | async-start | bytes 524288 | tf_op jit(solution)/shard_map/all_to_all | solution.py:11
  55.5 13.0 %all-to-all-start.1 = ((s32[16,16,6]{0,2,1:T(8,128)}), s32[16,16,6]{0,2,1:T(8,128)S(1)}, u32[]{:S(2)}, u32[]{:S(2)}) async-start(s32[16,16,6]{0,2,1:T(8,128)} %copy.177), calls=%async_computation.1 | async-start | bytes 131072 | tf_op jit(solution)/shard_map/all_to_all | solution.py:87
  68.5 87.6 %all-to-all-start.3 = ((bf16[16,16,6,1792]{3,0,2,1:T(8,128)(2,1)}), bf16[16,16,6,1792]{3,0,2,1:T(8,128)(2,1)}, u32[]{:S(2)}, u32[]{:S(2)}) async-start(bf16[16,16,6,1792]{3,0,2,1:T(8,128)(2,1)} %copy.185), calls=%async_computation.3 | async-start | bytes 11010048 | tf_op jit(solution)/shard_map/all_to_all | solution.py:80
  156.0 13.5 %all-to-all-start.2 = ((s32[16,16,6]{1,2,0:T(8,128)}), s32[16,16,6]{1,2,0:T(8,128)S(1)}, u32[]{:S(2)}, u32[]{:S(2)}) async-start(s32[16,16,6]{1,2,0:T(8,128)} %copy.178), calls=%async_computation.2 | async-start | bytes 131072 | tf_op jit(solution)/shard_map/all_to_all | solution.py:86
  169.5 129.0 %all-to-all-start.4 = ((bf16[16,16,6,1792]{3,1,2,0:T(8,128)(2,1)}), bf16[16,16,6,1792]{3,1,2,0:T(8,128)(2,1)}, u32[]{:S(2)}, u32[]{:S(2)}) async-start(bf16[16,16,6,1792]{3,1,2,0:T(8,128)(2,1)} %copy.186), calls=%async_computation.4 | async-start | bytes 11010048 | tf_op jit(solution)/shard_map/all_to_all | solution.py:79
  327.0 8.3 %copy-start = (bf16[1024,1792]{1,0:T(8,128)(2,1)S(1)}, bf16[1024,1792]{1,0:T(8,128)(2,1)}, u32[]{:S(2)}) copy-start(bf16[1024,1792]{1,0:T(8,128)(2,1)} %gather_fusion.1) | copy-start | bytes 11010052
  327.0 8.3 %copy-start.3 = (bf16[1,1792,1024]{2,1,0:T(8,128)(2,1)S(1)}, bf16[1,1792,1024]{2,1,0:T(8,128)(2,1)}, u32[]{:S(2)}) copy-start(bf16[1,1792,1024]{2,1,0:T(8,128)(2,1)} %param.9) | copy-start | bytes 11010052
  334.3 7.2 %collective-permute-start = (bf16[1024,1024]{1,0:T(8,128)(2,1)S(1)}, bf16[1024,1024]{1,0:T(8,128)(2,1)}, u32[]{:S(2)}, u32[]{:S(2)}) collective-permute-start(bf16[1024,1024]{1,0:T(8,128)(2,1)S(1)} %fusion.10), channel_id=1, source_target_pairs={{0,1},{1,0},{2,3},{3,2},{4,5},{5,4},{6,7},{7,6},{8,9},{9,8},{10,11... | collective-permute-start | bytes 6291464 | tf_op jit(solution)/shard_map/ppermute | solution.py:15
  340.9 4.7 collective-permute-start.1
  462.5 6.4 copy-start.1
  462.5 128.0 %all-to-all-start.6 = ((bf16[16,16,6,1792]{3,1,2,0:T(8,128)(2,1)}), bf16[16,16,6,1792]{3,1,2,0:T(8,128)(2,1)}, u32[]{:S(2)}, u32[]{:S(2)}) async-start(bf16[16,16,6,1792]{3,1,2,0:T(8,128)(2,1)} %copy.189), calls=%async_computation.6 | async-start | bytes 11010048 | tf_op jit(solution)/shard_map/all_to_all | solution.py:124
